TPU v7x, 32 devices: a whole 2x2x4 slice. The times are simulated.
32 devices in a mesh: dp: 4 (over z), ctx: 8 (over y, x, core).
Axes of the slice: x: 2, y: 2, z: 4, core: 2. Of those that a mesh axis runs over, the one named last changes fastest.
Arguments:
- output_gate_input: bfloat16 [4, 1024, 4096], P('dp', 'ctx'), may hold values from -6 to 6
- key_input: bfloat16 [4, 1024, 4096], P('dp', 'ctx'), may hold values from -6 to 6
- value_input: bfloat16 [4, 1024, 4096], P('dp', 'ctx'), may hold values from -6 to 6
- upstream: bfloat16 [4, 1024, 4096], P('dp', 'ctx'), may hold values from -6 to 6
- filter_taps: float32 [256, 1024], P('ctx'), may hold values from -6 to 6
- block_of_shard: int32 [8], replicated, may hold values from 0 to 7, each once
Outputs:
- mixed_out: bfloat16 [4, 1024, 4096], P('dp', 'ctx')
- gate_grad: bfloat16 [4, 1024, 4096], P('dp', 'ctx')
- key_grad: bfloat16 [4, 1024, 4096], P('dp', 'ctx')
- value_grad: bfloat16 [4, 1024, 4096], P('dp', 'ctx')
- taps_grad: float32 [256, 1024], P('ctx')
Inputs may be any that keep to these rules, and one draw needn't show every extreme that they name: block_of_shard names every block of positions exactly once.
All inputs are finite; a program needn't handle non-finite values.
Results may differ from a plain program's by a relative error of at most 0.012.
Values may be sent and summed in bfloat16 or wider, within the bound.
A program may use at most 192 MiB of HBM per device.

v0:
```python
import functools
import math

import jax
import jax.numpy as jnp
from jax import lax
from jax.experimental import pallas as pl
from jax.experimental.pallas import tpu as pltpu
from jax.sharding import PartitionSpec as P

epsilon = 1e-06
F32 = jnp.float32
BF16 = jnp.bfloat16
EARLY = 2


def gate_product(first, second):
    return (first.astype(F32) * second.astype(F32)).astype(BF16)


def toeplitz_table(row, rows):
    length = row.shape[1]
    spread = jnp.broadcast_to(row, (rows, length))
    rolled = pltpu.roll(spread, 0, 1, stride=1, stride_axis=0)
    lag = lax.broadcasted_iota(jnp.int32, (rows, rows), 1) - lax.broadcasted_iota(
        jnp.int32, (rows, rows), 0
    )
    first = jnp.where(lag >= 0, rolled[:, :rows], 0.0)
    return jnp.concatenate([first, rolled[:, rows:]], axis=1).astype(BF16)


def diagonal_sums(square):
    rows, length = square.shape
    total_index = lax.broadcasted_iota(jnp.int32, (rows, rows), 0) + lax.broadcasted_iota(
        jnp.int32, (rows, rows), 1
    )
    last = jnp.where(total_index < rows, square[:, length - rows :], 0.0)
    total = jnp.concatenate([square[:, : length - rows], last], axis=1)
    half = rows // 2
    while half >= 8:
        total = total[:half] + pltpu.roll(total[half:], half, 1)
        half //= 2
    while half >= 1:
        total = total + pltpu.roll(pltpu.roll(total, half, 1), 8 - half, 0)
        half //= 2
    return total[:1]


def turning(rows, kind):
    total_index = lax.broadcasted_iota(jnp.int32, (rows, rows), 0) + lax.broadcasted_iota(
        jnp.int32, (rows, rows), 1
    )
    return jnp.where(total_index == rows - 1, 1.0, 0.0).astype(kind)


def group_work(signal, weighted, table, pieces):
    lines, rows = signal.shape
    size = lines // pieces

    def later(l):
        return jnp.concatenate([jnp.zeros((l * size, rows), BF16), signal[: lines - l * size]], axis=0) if l else signal

    def earlier(l):
        return jnp.concatenate([weighted[l * size :], jnp.zeros((l * size, rows), BF16)], axis=0) if l else weighted

    ahead = [earlier(l) for l in range(pieces)]
    both = jnp.concatenate(
        [jnp.concatenate([later(l), ahead[l]], axis=0) for l in range(pieces)], axis=1
    )
    stacked = jnp.concatenate(
        [table[:, l * rows : (l + 1) * rows] for l in range(pieces)], axis=0
    )
    filtered = jnp.dot(both, stacked, preferred_element_type=F32).astype(BF16)
    square = lax.dot_general(
        signal,
        jnp.concatenate(ahead[::-1], axis=1),
        (((0,), (0,)), ((), ())),
        preferred_element_type=F32,
    )
    return filtered[:lines], filtered[lines:], diagonal_sums(square)


def scale_of(taps):
    mean = jnp.mean(taps * taps, axis=1, keepdims=True)
    return 1.0 / (math.sqrt(taps.shape[1]) * jnp.sqrt(mean + epsilon))


def layer(
    waves, pieces, copies,
    block_ref, taps_ref, gates_ref, keys_ref, values_ref, grads_ref,
    mixing_ref, returned_ref, taps_grad_ref,
    places_ref, tables_ref, ordered_ref, filtered_ref, *rest,
):
    sends, recvs, results, homes, lags = (rest[i * waves : (i + 1) * waves] for i in range(5))
    out_sem, in_sem, back_sem, home_sem, lag_out_sem, lag_in_sem = rest[5 * waves :]
    me = lax.axis_index("ctx")
    me_dp = lax.axis_index("dp")
    rows, width = gates_ref.shape
    channels = width // pieces
    part = channels // waves
    groups = taps_ref.shape[0]
    size = channels // groups
    each = groups // waves
    turn = turning(rows, BF16)
    pair = 2 if pieces <= 8 and each % 2 == 0 else 1

    barrier = pltpu.get_barrier_semaphore()

    @pl.loop(1, pieces)
    def _(o):
        pl.semaphore_signal(
            barrier, inc=1, device_id={"ctx": lax.rem(me + o, pieces)}, device_id_type=pl.DeviceIdType.MESH
        )

    @pl.loop(1, copies)
    def _(o):
        pl.semaphore_signal(
            barrier, inc=1, device_id={"dp": lax.rem(me_dp + o, copies)}, device_id_type=pl.DeviceIdType.MESH
        )

    def prepare(w, d, ref, slot):
        columns = pl.ds(pl.multiple_of(d * channels + w * part, 128), part)
        ref[slot, 0] = gate_product(keys_ref[:, columns], values_ref[:, columns]).T
        ref[slot, 1] = lax.dot_general(
            gate_product(grads_ref[:, columns], gates_ref[:, columns]), turn,
            (((0,), (0,)), ((), ())), preferred_element_type=F32,
        ).astype(BF16)

    def outward(w, d):
        return pltpu.make_async_remote_copy(
            src_ref=sends[w].at[d], dst_ref=recvs[w].at[me],
            send_sem=out_sem.at[w, d], recv_sem=in_sem.at[w, me],
            device_id={"ctx": d}, device_id_type=pl.DeviceIdType.MESH,
        )

    def inward(w, d):
        return pltpu.make_async_remote_copy(
            src_ref=sends[w].at[d], dst_ref=recvs[w].at[d],
            send_sem=out_sem.at[w, d], recv_sem=in_sem.at[w, d],
            device_id={"ctx": d}, device_id_type=pl.DeviceIdType.MESH,
        )

    def homeward(w, d):
        return pltpu.make_async_remote_copy(
            src_ref=results[w].at[d], dst_ref=homes[w].at[me],
            send_sem=back_sem.at[w, d], recv_sem=home_sem.at[w, me],
            device_id={"ctx": d}, device_id_type=pl.DeviceIdType.MESH,
        )

    def arriving(w, d):
        return pltpu.make_async_remote_copy(
            src_ref=results[w].at[d], dst_ref=homes[w].at[d],
            send_sem=back_sem.at[w, d], recv_sem=home_sem.at[w, d],
            device_id={"ctx": d}, device_id_type=pl.DeviceIdType.MESH,
        )

    def lag_copy(w, d, slot):
        return pltpu.make_async_remote_copy(
            src_ref=lags[w].at[me_dp], dst_ref=lags[w].at[slot],
            send_sem=lag_out_sem.at[w, d], recv_sem=lag_in_sem.at[w, slot],
            device_id={"dp": d}, device_id_type=pl.DeviceIdType.MESH,
        )

    @pl.loop(1, pieces)
    def _(o):
        d = lax.rem(me + o, pieces)
        prepare(0, d, sends[0], d)

    pl.semaphore_wait(barrier, pieces + copies - 2)

    @pl.loop(1, pieces)
    def _(o):
        outward(0, lax.rem(me + o, pieces)).start()

    for w in range(1, waves):

        @pl.loop(1, pieces)
        def _(o):
            d = lax.rem(me + o, pieces)
            prepare(w, d, sends[w], d)
            outward(w, d).start()

    for w in range(waves):
        prepare(w, me, recvs[w], me)

    @pl.loop(0, pieces)
    def _(b):
        found = 0
        for d in range(pieces):
            found = jnp.where(block_ref[d] == b, d, found)
        places_ref[b] = found

    def build(g):
        taps = taps_ref[pl.ds(g, 1), :]
        kernel = (taps * scale_of(taps)).astype(BF16).astype(F32)
        return toeplitz_table(kernel, rows)

    early = min(EARLY, waves)

    @pl.loop(0, early * each // pair)
    def _(i):
        made = [build(i * pair + k) for k in range(pair)]
        for k in range(pair):
            tables_ref[i * pair + k] = made[k]

    def unload(w):
        @pl.loop(1, pieces)
        def _(o):
            arriving(w, lax.rem(me + pieces - o, pieces)).wait_recv()

        @pl.loop(0, pieces)
        def _(d):
            columns = pl.ds(pl.multiple_of(d * channels + w * part, 128), part)
            mixing_ref[:, columns] = homes[w][d, 0].T
            returned_ref[:, columns] = lax.dot_general(
                turn, homes[w][d, 1], (((1,), (1,)), ((), ())), preferred_element_type=F32
            ).astype(BF16)

    for w in range(waves):

        @pl.loop(1, pieces)
        def _(o):
            inward(w, lax.rem(me + pieces - o, pieces)).wait_recv()

        @pl.loop(0, pieces)
        def _(b):
            ordered_ref[b] = recvs[w][places_ref[b]]

        @pl.loop(0, each // pair)
        def _(i):
            made = []
            for k in range(pair):
                g = i * pair + k
                table = tables_ref[w * each + g] if w < early else build(w * each + g)
                lines = pl.ds(pl.multiple_of(g * size, size), size)
                signal = ordered_ref[:, 0, lines, :].reshape(pieces * size, rows)
                weighted = ordered_ref[:, 1, lines, :].reshape(pieces * size, rows)
                made.append((g, lines, *group_work(signal, weighted, table, pieces)))
            for g, lines, mixing, returned, sums in made:
                filtered_ref[:, 0, lines, :] = mixing.reshape(pieces, size, rows)
                filtered_ref[:, 1, lines, :] = returned.reshape(pieces, size, rows)
                lags[w][me_dp, pl.ds(g, 1), :] = sums

        @pl.loop(0, pieces)
        def _(d):
            results[w][d] = filtered_ref[block_ref[d]]

        @pl.loop(1, pieces)
        def _(o):
            homeward(w, lax.rem(me + o, pieces)).start()

        @pl.loop(1, copies)
        def _(o):
            lag_copy(w, lax.rem(me_dp + o, copies), me_dp).start()

        homes[w][me] = results[w][me]
        if w > 0:
            unload(w - 1)

    def finish(w):
        @pl.loop(1, copies)
        def _(o):
            d = lax.rem(me_dp + copies - o, copies)
            lag_copy(w, d, d).wait_recv()

        total = lags[w][0]
        for i in range(1, copies):
            total = total + lags[w][i]
        turned = turning(rows, F32)
        mean = jnp.concatenate(
            [
                jnp.dot(
                    total[:, l * rows : (l + 1) * rows], turned,
                    precision=lax.Precision.HIGHEST, preferred_element_type=F32,
                )
                for l in reversed(range(pieces))
            ],
            axis=1,
        ) / copies
        taps = taps_ref[w * each : (w + 1) * each, :]
        scale = scale_of(taps)
        projection = jnp.sum(mean * taps, axis=1, keepdims=True)
        taps_grad_ref[w * each : (w + 1) * each, :] = (
            scale * mean - taps * (scale * scale * scale) * projection
        )

    for w in range(waves - 1):
        finish(w)
    unload(waves - 1)
    finish(waves - 1)

    for w in range(waves):

        @pl.loop(1, pieces)
        def _(o):
            d = lax.rem(me + o, pieces)
            outward(w, d).wait_send()
            homeward(w, d).wait_send()

        @pl.loop(1, copies)
        def _(o):
            lag_copy(w, lax.rem(me_dp + o, copies), me_dp).wait_send()


def shards(output_gate_input, key_input, value_input, upstream, filter_taps, block_of_shard):
    groups, length = filter_taps.shape
    pieces = block_of_shard.shape[0]
    copies = lax.axis_size("dp")
    gates, keys, values, grads = (
        member[0] for member in (output_gate_input, key_input, value_input, upstream)
    )
    rows, width = gates.shape
    channels = width // pieces
    part = 128
    waves = channels // part
    each = groups // waves
    vmem = pl.BlockSpec(memory_space=pltpu.VMEM)
    smem = pl.BlockSpec(memory_space=pltpu.SMEM)
    slots = pltpu.VMEM((pieces, 2, part, rows), BF16)
    ctx_sems = pltpu.SemaphoreType.DMA((waves, pieces))
    dp_sems = pltpu.SemaphoreType.DMA((waves, copies))
    mixing, returned, taps_grad = pl.pallas_call(
        functools.partial(layer, waves, pieces, copies),
        out_shape=(
            jax.ShapeDtypeStruct((rows, width), BF16),
            jax.ShapeDtypeStruct((rows, width), BF16),
            jax.ShapeDtypeStruct((groups, length), F32),
        ),
        in_specs=[smem] + [vmem] * 5,
        out_specs=(vmem,) * 3,
        scratch_shapes=[
            pltpu.SMEM((pieces,), jnp.int32),
            pltpu.VMEM((min(EARLY, waves) * each, rows, length), BF16),
            slots,
            slots,
            *([slots] * (4 * waves)),
            *([pltpu.VMEM((copies, each, length), F32)] * waves),
            ctx_sems, ctx_sems, ctx_sems, ctx_sems, dp_sems, dp_sems,
        ],
        compiler_params=pltpu.CompilerParams(
            vmem_limit_bytes=56 * 1024 * 1024, collective_id=0, has_side_effects=True
        ),
        cost_estimate=pl.CostEstimate(
            flops=6 * channels * length * length, bytes_accessed=12 * rows * width, transcendentals=0
        ),
    )(block_of_shard, filter_taps, gates, keys, values, grads)
    return (
        gate_product(gates, mixing)[None],
        gate_product(grads, mixing)[None],
        gate_product(returned, values)[None],
        gate_product(returned, keys)[None],
        taps_grad,
    )


def solution(mesh):
    wide = P("dp", "ctx", None)
    return jax.shard_map(
        shards,
        mesh=mesh,
        in_specs=(wide, wide, wide, wide, P("ctx", None), P()),
        out_specs=(wide, wide, wide, wide, P("ctx", None)),
        check_vma=False,
    )
```

profile of v0, /device:TPU:1, one launch (start us, length us, event | category | flops | bytes accessed | tf_op | source)
XLA Modules:
  0.0 70.1 jit_solution(9094482912745934659)
XLA Ops:
  0.6 0.0 copy-start
  0.6 0.0 copy-start.1
  0.7 0.0 copy-start.2
  0.7 0.0 copy-start.3
  0.7 64.0 %shard_map.101 = (bf16[128,4096]{1,0:T(8,128)(2,1)}, bf16[128,4096]{1,0:T(8,128)(2,1)}, f32[32,1024]{1,0:T(8,128)}) custom-call(s32[8]{0:T(128)} %block_ref.1, f32[32,1024]{1,0:T(8,128)} %taps_ref.1, bf16[128,4096]{1,0:T(8,128)(2,1)} %bitcast.16, bf16[128,4096]{1,0:T(8,128)(2,1)} %bitcast.17, bf16[128,4096]{1,0:T(8,128)(2,1)} %bitcast.18, ...), custom_call_target="tpu_custom_call" | custom-call | flops 3221225472 | bytes 6291456 | tf_op jit(solution)/shard_map/pallas_call | solution.py:322
  64.7 0.0 copy-done
  64.7 0.0 copy-done.1
  64.7 0.0 copy-done.2
  64.7 0.0 copy-done.3
  64.7 0.0 copy-start.4
  64.7 4.7 %fusion.4 = (bf16[1,128,4096]{2,1,0:T(8,128)(2,1)}, bf16[1,128,4096]{2,1,0:T(8,128)(2,1)}, bf16[1,128,4096]{2,1,0:T(8,128)(2,1)}, bf16[1,128,4096]{2,1,0:T(8,128)(2,1)}) fusion(bf16[128,4096]{1,0:T(8,128)(2,1)} %get-tuple-element.9, bf16[1,128,4096]{2,1,0:T(8,128)(2,1)S(1)} %copy-done.1, bf16[1,128,4096]{2,1,0:T(8,128)(2,1)S(1)} %copy-done.2, ...), kind=kLoop, calls=%fused_computation.8 | loop fusion | flops 7340032 | bytes 10485760 | tf_op jit(solution)/shard_map/broadcast_in_dim | solution.py:351
  69.4 0.0 copy-done.4
  69.4 0.7 copy.12
Async XLA Ops:
  0.6 64.0 %copy-start = (bf16[1,128,4096]{2,1,0:T(8,128)(2,1)S(1)}, bf16[1,128,4096]{2,1,0:T(8,128)(2,1)}, u32[]{:S(2)}) copy-start(bf16[1,128,4096]{2,1,0:T(8,128)(2,1)} %param.6) | copy-start | bytes 3145732
  0.6 64.0 %copy-start.1 = (bf16[1,128,4096]{2,1,0:T(8,128)(2,1)S(1)}, bf16[1,128,4096]{2,1,0:T(8,128)(2,1)}, u32[]{:S(2)}) copy-start(bf16[1,128,4096]{2,1,0:T(8,128)(2,1)} %param.7) | copy-start | bytes 3145732
  0.7 64.0 %copy-start.2 = (bf16[1,128,4096]{2,1,0:T(8,128)(2,1)S(1)}, bf16[1,128,4096]{2,1,0:T(8,128)(2,1)}, u32[]{:S(2)}) copy-start(bf16[1,128,4096]{2,1,0:T(8,128)(2,1)} %param.8) | copy-start | bytes 3145732
  0.7 64.0 %copy-start.3 = (bf16[1,128,4096]{2,1,0:T(8,128)(2,1)S(1)}, bf16[1,128,4096]{2,1,0:T(8,128)(2,1)}, u32[]{:S(2)}) copy-start(bf16[1,128,4096]{2,1,0:T(8,128)(2,1)} %param.9) | copy-start | bytes 3145732
  64.7 4.7 %copy-start.4 = (f32[32,1024]{1,0:T(8,128)S(1)}, f32[32,1024]{1,0:T(8,128)}, u32[]{:S(2)}) copy-start(f32[32,1024]{1,0:T(8,128)} %get-tuple-element.26) | copy-start | bytes 393220
where the time goes:
time: 70.2 us; the launch traced here: 70.1 us
  Pallas kernels  64 us (91%)
  other arithmetic  4.69 us (7%)
  between operations  0.71 us (1%)
    pallas_call x1, Pallas kernels, shards(): pl.pallas_call(functools.partial(layer, waves, pieces, copies), out_shape...  64 us
    broadcast_in_dim x1, other arithmetic, shards(): gate_product(returned, keys)[None]  4.69 us

commit v1 on v0

--- a/solution.py
+++ b/solution.py
@@ -15,7 +15,7 @@
 
 
 def gate_product(first, second):
-    return (first.astype(F32) * second.astype(F32)).astype(BF16)
+    return first * second
 
 
 def toeplitz_table(row, rows):
@@ -83,6 +83,37 @@
 def scale_of(taps):
     mean = jnp.mean(taps * taps, axis=1, keepdims=True)
     return 1.0 / (math.sqrt(taps.shape[1]) * jnp.sqrt(mean + epsilon))
+
+
+def exclusive_or(first, second, size):
+    total, bit = 0, 1
+    while bit < size:
+        total = total + bit * lax.rem(first // bit + second // bit, 2)
+        bit *= 2
+    return total
+
+
+def send_orders(pieces):
+    half = pieces // 2
+    chips = list(range(1, half))
+    turned = [chips[1], chips[0], *chips[2:]] if len(chips) > 1 else chips
+    one = [2 * c for c in chips] + [2 * c + 1 for c in chips] + [1]
+    other = [2 * c + 1 for c in turned] + [2 * c for c in turned] + [1]
+    return list(zip(one, other))
+
+
+def partners(me, pieces):
+    core = lax.rem(me, 2)
+    for one, other in send_orders(pieces):
+        yield exclusive_or(me, one + core * (other - one), pieces)
+
+
+def products(gates, grads, keys, values, mixing, returned, taps, out, gate, key, value, taps_out):
+    out[...] = gates[...] * mixing[...]
+    gate[...] = grads[...] * mixing[...]
+    key[...] = returned[...] * values[...]
+    value[...] = returned[...] * keys[...]
+    taps_out[...] = taps[...]
 
 
 def layer(
@@ -163,21 +194,21 @@
 
     @pl.loop(1, pieces)
     def _(o):
-        d = lax.rem(me + o, pieces)
+        d = exclusive_or(me, o, pieces)
         prepare(0, d, sends[0], d)
 
     pl.semaphore_wait(barrier, pieces + copies - 2)
 
-    @pl.loop(1, pieces)
-    def _(o):
-        outward(0, lax.rem(me + o, pieces)).start()
+    for d in partners(me, pieces):
+        outward(0, d).start()
 
     for w in range(1, waves):
-
         @pl.loop(1, pieces)
         def _(o):
-            d = lax.rem(me + o, pieces)
+            d = exclusive_or(me, o, pieces)
             prepare(w, d, sends[w], d)
+
+        for d in partners(me, pieces):
             outward(w, d).start()
 
     for w in range(waves):
@@ -245,9 +276,8 @@
         def _(d):
             results[w][d] = filtered_ref[block_ref[d]]
 
-        @pl.loop(1, pieces)
-        def _(o):
-            homeward(w, lax.rem(me + o, pieces)).start()
+        for d in partners(me, pieces):
+            homeward(w, d).start()
 
         @pl.loop(1, copies)
         def _(o):
@@ -344,13 +374,19 @@
             flops=6 * channels * length * length, bytes_accessed=12 * rows * width, transcendentals=0
         ),
     )(block_of_shard, filter_taps, gates, keys, values, grads)
-    return (
-        gate_product(gates, mixing)[None],
-        gate_product(grads, mixing)[None],
-        gate_product(returned, values)[None],
-        gate_product(returned, keys)[None],
-        taps_grad,
-    )
+    steps = 4
+    wide = pl.BlockSpec((rows // steps, width), lambda i: (i, 0))
+    whole = pl.BlockSpec((groups, length), lambda i: (0, 0))
+    *outs, taps_grad = pl.pallas_call(
+        products,
+        grid=(steps,),
+        out_shape=[jax.ShapeDtypeStruct((rows, width), BF16)] * 4
+        + [jax.ShapeDtypeStruct((groups, length), F32)],
+        in_specs=[wide] * 6 + [whole],
+        out_specs=[wide] * 4 + [whole],
+        compiler_params=pltpu.CompilerParams(vmem_limit_bytes=32 * 1024 * 1024),
+    )(gates, grads, keys, values, mixing, returned, taps_grad)
+    return (*(out[None] for out in outs), taps_grad)
 
 
 def solution(mesh):

time: 70.2 us -> 69.6 us (level)
  other arithmetic: 4.69 us -> 0 us
  local copies, waits for them, and re-layouts: 0.68 us -> 3.36 us
  Pallas kernels: 64 us -> 65.3 us
    broadcast_in_dim x1 -> x0, other arithmetic: 4.69 us -> none  [shards(): gate_product(returned, keys)[None]]
    unnamed x11 -> x14, local copies, waits for them, and re-layouts: 0.68 us -> 3.36 us
    pallas_call x0 -> x1, Pallas kernels: none -> 2.52 us  [shards(): pl.pallas_call(products, grid=(steps,), out_shape=[jax.ShapeDtypeStruct((...]
    pallas_call x1, Pallas kernels: 64 us -> 62.7 us  [shards(): pl.pallas_call(functools.partial(layer, waves, pieces, copies), out_shape...]
where the time goes in v1:
time: 69.6 us; the launch traced here: 69.3 us
  Pallas kernels  65.3 us (94%)
  local copies, waits for them, and re-layouts  3.36 us (5%)
  between operations  0.71 us (1%)
    pallas_call x1, Pallas kernels, shards(): pl.pallas_call(functools.partial(layer, waves, pieces, copies), out_shape...  62.7 us
    unnamed x14, local copies, waits for them, and re-layouts  3.36 us
    pallas_call x1, Pallas kernels, shards(): pl.pallas_call(products, grid=(steps,), out_shape=[jax.ShapeDtypeStruct((...  2.52 us

profile of v1, /device:TPU:1, one launch (start us, length us, event | category | flops | bytes accessed | tf_op | source)
XLA Modules:
  0.0 69.3 jit_solution(14698778196965110681)
XLA Ops:
  0.6 0.0 copy-start
  0.6 0.0 copy-start.1
  0.7 0.0 copy-start.2
  0.7 0.0 copy-start.3
  0.7 62.7 %shard_map.101 = (bf16[128,4096]{1,0:T(8,128)(2,1)}, bf16[128,4096]{1,0:T(8,128)(2,1)}, f32[32,1024]{1,0:T(8,128)}) custom-call(s32[8]{0:T(128)} %block_ref.1, f32[32,1024]{1,0:T(8,128)} %taps_ref.1, bf16[128,4096]{1,0:T(8,128)(2,1)} %bitcast.8, bf16[128,4096]{1,0:T(8,128)(2,1)} %bitcast.12, bf16[128,4096]{1,0:T(8,128)(2,1)} %bitcast.14, ...), custom_call_target="tpu_custom_call" | custom-call | flops 3221225472 | bytes 6291456 | tf_op jit(solution)/shard_map/pallas_call | solution.py:352
  63.4 0.0 copy-done
  63.4 0.0 copy-done.1
  63.4 0.0 copy-done.2
  63.5 0.0 copy-done.3
  63.5 0.0 copy-start.4
  63.5 1.2 %copy-done.4 = bf16[128,4096]{1,0:T(8,128)(2,1)S(1)} copy-done((bf16[128,4096]{1,0:T(8,128)(2,1)S(1)}, bf16[128,4096]{1,0:T(8,128)(2,1)}, u32[]{:S(2)}) %copy-start.4) | copy-done | bytes 1048600
  64.7 0.0 copy-start.5
  64.7 1.2 %copy-done.5 = bf16[128,4096]{1,0:T(8,128)(2,1)S(1)} copy-done((bf16[128,4096]{1,0:T(8,128)(2,1)S(1)}, bf16[128,4096]{1,0:T(8,128)(2,1)}, u32[]{:S(2)}) %copy-start.5) | copy-done | bytes 1048600
  65.9 0.0 copy-start.6
  65.9 0.9 %copy-done.6 = f32[32,1024]{1,0:T(8,128)S(1)} copy-done((f32[32,1024]{1,0:T(8,128)S(1)}, f32[32,1024]{1,0:T(8,128)}, u32[]{:S(2)}) %copy-start.6) | copy-done | bytes 131096
  66.8 2.5 %shard_map.102 = (bf16[128,4096]{1,0:T(8,128)(2,1)}, bf16[128,4096]{1,0:T(8,128)(2,1)}, bf16[128,4096]{1,0:T(8,128)(2,1)}, bf16[128,4096]{1,0:T(8,128)(2,1)}, f32[32,1024]{1,0:T(8,128)}) custom-call(bf16[128,4096]{1,0:T(8,128)(2,1)S(1)} %bitcast.9, bf16[128,4096]{1,0:T(8,128)(2,1)S(1)} %bitcast.11, bf16[128,4096]{1,0:T(8,128)(2,1)S(1)} %bitcast.13, ...), custom_call_target="tpu_custom_call" | custom-call | tf_op jit(solution)/shard_map/pallas_call | solution.py:380
Async XLA Ops:
  0.6 62.8 %copy-start = (bf16[1,128,4096]{2,1,0:T(8,128)(2,1)S(1)}, bf16[1,128,4096]{2,1,0:T(8,128)(2,1)}, u32[]{:S(2)}) copy-start(bf16[1,128,4096]{2,1,0:T(8,128)(2,1)} %param.6) | copy-start | bytes 3145732
  0.6 62.8 %copy-start.1 = (bf16[1,128,4096]{2,1,0:T(8,128)(2,1)S(1)}, bf16[1,128,4096]{2,1,0:T(8,128)(2,1)}, u32[]{:S(2)}) copy-start(bf16[1,128,4096]{2,1,0:T(8,128)(2,1)} %param.9) | copy-start | bytes 3145732
  0.7 62.8 %copy-start.2 = (bf16[1,128,4096]{2,1,0:T(8,128)(2,1)S(1)}, bf16[1,128,4096]{2,1,0:T(8,128)(2,1)}, u32[]{:S(2)}) copy-start(bf16[1,128,4096]{2,1,0:T(8,128)(2,1)} %param.7) | copy-start | bytes 3145732
  0.7 62.8 %copy-start.3 = (bf16[1,128,4096]{2,1,0:T(8,128)(2,1)S(1)}, bf16[1,128,4096]{2,1,0:T(8,128)(2,1)}, u32[]{:S(2)}) copy-start(bf16[1,128,4096]{2,1,0:T(8,128)(2,1)} %param.8) | copy-start | bytes 3145732
  63.5 1.2 %copy-start.4 = (bf16[128,4096]{1,0:T(8,128)(2,1)S(1)}, bf16[128,4096]{1,0:T(8,128)(2,1)}, u32[]{:S(2)}) copy-start(bf16[128,4096]{1,0:T(8,128)(2,1)} %get-tuple-element.13.mixing) | copy-start | bytes 3145732
  64.7 1.2 %copy-start.5 = (bf16[128,4096]{1,0:T(8,128)(2,1)S(1)}, bf16[128,4096]{1,0:T(8,128)(2,1)}, u32[]{:S(2)}) copy-start(bf16[128,4096]{1,0:T(8,128)(2,1)} %get-tuple-element.14.returned) | copy-start | bytes 3145732
  65.9 0.9 %copy-start.6 = (f32[32,1024]{1,0:T(8,128)S(1)}, f32[32,1024]{1,0:T(8,128)}, u32[]{:S(2)}) copy-start(f32[32,1024]{1,0:T(8,128)} %get-tuple-element.15.taps) | copy-start | bytes 393220
